TPU v7x, 32 devices: a whole 2x2x4 slice. The times are simulated.
32 devices in a mesh: qrow: 8 (over y, x, core), kcol: 4 (over z).
Axes of the slice: x: 2, y: 2, z: 4, core: 2. Of those that a mesh axis runs over, the one named last changes fastest.
Arguments:
- queries: bfloat16 [4096, 1024], P(('qrow', 'kcol')), may hold values from -6 to 6
- keys: bfloat16 [4096, 128], P(('qrow', 'kcol')), may hold values from -6 to 6
- values: bfloat16 [4096, 128], P(('qrow', 'kcol')), may hold values from -6 to 6
- grad_out: bfloat16 [4096, 1024], P(('qrow', 'kcol')), may hold values from -96 to 96
- block_order: int32 [32], replicated, may hold values from 0 to 31, each once
Outputs:
- grad_queries: bfloat16 [4096, 1024], P(('qrow', 'kcol'))
- grad_keys: bfloat16 [4096, 128], P(('qrow', 'kcol'))
- grad_values: bfloat16 [4096, 128], P(('qrow', 'kcol'))
Inputs may be any that keep to these rules, and one draw needn't show every extreme that they name: `block_order`: each of the 32 block numbers appears once.
All inputs are finite; a program needn't handle non-finite values.
Results may differ from a plain program's by a relative error of at most 0.0076.
Values may be sent and summed in bfloat16 or wider, within the bound.
A program may use at most 128 MiB of HBM per device.

v0:
```python
import math

import jax
import jax.numpy as jnp
from jax import lax
from jax.sharding import PartitionSpec as P

HD = 128


NEG = -1e30


def lookup(table, wanted):
    hits = wanted[:, None] == jnp.arange(table.shape[0], dtype=jnp.int32)[None, :]
    return jnp.sum(jnp.where(hits, table[None, :], 0), axis=1)


def spread_positions(blocks, length):
    return (blocks[:, None] * length + jnp.arange(length, dtype=jnp.int32)[None, :]).reshape(-1)


def head_stats(visible, masked, grad_weights):
    local_top = jnp.max(masked, axis=1)
    top = lax.pmax(local_top, "qrow")
    raised = jnp.where(visible, jnp.exp(masked - top[:, None]), 0.0)
    total, moment = lax.psum(
        (jnp.sum(raised, axis=1), jnp.sum(raised * grad_weights, axis=1)), "qrow"
    )
    attention = jnp.where(visible, jnp.exp(masked - top[:, None]), 0.0) / total[:, None]
    return (attention, moment / total)


def tile_backward(query_block, grad_block, key_block, value_block, query_positions, key_positions):
    heads = query_block.shape[1] // HD
    inverse_root = 1.0 / math.sqrt(HD)
    visible = key_positions[None, :] <= query_positions[:, None]

    def per_head(carry, head_index):
        query_sum, key_sum, value_sum = carry
        query_head = lax.dynamic_slice_in_dim(query_block, head_index * HD, HD, 1)
        grad_head = lax.dynamic_slice_in_dim(grad_block, head_index * HD, HD, 1)
        scores = (
            jnp.einsum("qd,kd->qk", query_head, key_block, preferred_element_type=jnp.float32)
            * inverse_root
        )
        grad_weights = jnp.einsum(
            "qd,kd->qk", grad_head, value_block, preferred_element_type=jnp.float32
        )
        masked = jnp.where(visible, scores, NEG)
        attention, delta = head_stats(visible, masked, grad_weights)
        attention_low = attention.astype(jnp.bfloat16)
        grad_scores = (attention * (grad_weights - delta[:, None])).astype(jnp.bfloat16)
        value_sum = value_sum + jnp.einsum(
            "qk,qd->kd", attention_low, grad_head, preferred_element_type=jnp.float32
        )
        key_sum = (
            key_sum
            + jnp.einsum("qk,qd->kd", grad_scores, query_head, preferred_element_type=jnp.float32)
            * inverse_root
        )
        grad_query = (
            jnp.einsum("qk,kd->qd", grad_scores, key_block, preferred_element_type=jnp.float32)
            * inverse_root
        )
        query_sum = lax.dynamic_update_slice_in_dim(query_sum, grad_query, head_index * HD, 1)
        return ((query_sum, key_sum, value_sum), None)

    start = (
        jnp.zeros(query_block.shape, jnp.float32),
        jnp.zeros(key_block.shape, jnp.float32),
        jnp.zeros(value_block.shape, jnp.float32),
    )
    result, unused = lax.scan(per_head, start, jnp.arange(heads, dtype=jnp.int32))
    return result


def per_device(queries, keys, values, grad_out, block_order):
    length = queries.shape[0]
    rows_count = lax.axis_size("qrow")
    cols_count = lax.axis_size("kcol")
    row_index = lax.axis_index("qrow")
    col_index = lax.axis_index("kcol")
    query_block, grad_block = (
        lax.all_gather(queries, "qrow", axis=0, tiled=True),
        lax.all_gather(grad_out, "qrow", axis=0, tiled=True),
    )
    key_block, value_block = (
        lax.all_gather(keys, "kcol", axis=0, tiled=True),
        lax.all_gather(values, "kcol", axis=0, tiled=True),
    )
    query_ids = jnp.arange(rows_count, dtype=jnp.int32) * cols_count + col_index
    key_ids = row_index * cols_count + jnp.arange(cols_count, dtype=jnp.int32)
    query_positions = spread_positions(lookup(block_order, query_ids), length)
    key_positions = spread_positions(lookup(block_order, key_ids), length)
    query_sum, key_sum, value_sum = tile_backward(
        query_block, grad_block, key_block, value_block, query_positions, key_positions
    )
    grad_queries = lax.psum_scatter(query_sum, "qrow", scatter_dimension=0, tiled=True)
    grad_keys, grad_values = (
        lax.psum_scatter(key_sum, "kcol", scatter_dimension=0, tiled=True),
        lax.psum_scatter(value_sum, "kcol", scatter_dimension=0, tiled=True),
    )
    return (
        grad_queries.astype(jnp.bfloat16),
        grad_keys.astype(jnp.bfloat16),
        grad_values.astype(jnp.bfloat16),
    )


def solution(mesh):
    return jax.shard_map(
        per_device,
        mesh=mesh,
        in_specs=(
            P(("qrow", "kcol"), None),
            P(("qrow", "kcol"), None),
            P(("qrow", "kcol"), None),
            P(("qrow", "kcol"), None),
            P(),
        ),
        out_specs=(P(("qrow", "kcol"), None), P(("qrow", "kcol"), None), P(("qrow", "kcol"), None)),
        check_vma=False,
    )
```

profile of v0, /device:TPU:0, one launch (start us, length us, event | category | flops | bytes accessed | tf_op | source)
XLA Modules:
  0.0 469.6 jit_solution(9026991278920529075)
XLA Ops:
  8.7 15.3 %all_gather.13 = bf16[512,128]{1,0:T(8,128)(2,1)S(1)} all-gather(bf16[128,128]{1,0:T(8,128)(2,1)} %param.8), channel_id=1, replica_groups=mesh['qrow'=8,'kcol'=4] {'kcol'}, dimensions={0}, use_global_device_ids=true | all-gather | bytes 163840 | tf_op jit(solution)/shard_map/all_gather | solution.py:89
  24.0 13.8 %all_gather.15 = bf16[512,128]{1,0:T(8,128)(2,1)S(1)} all-gather(bf16[128,128]{1,0:T(8,128)(2,1)} %param.9), channel_id=1, replica_groups=mesh['qrow'=8,'kcol'=4] {'kcol'}, dimensions={0}, use_global_device_ids=true | all-gather | bytes 163840 | tf_op jit(solution)/shard_map/all_gather | solution.py:90
  40.5 29.8 %all-gather.5.cloned.1.call-done = bf16[1024,1024]{1,0:T(8,128)(2,1)} async-done(((bf16[128,1024]{1,0:T(8,128)(2,1)}), bf16[1024,1024]{1,0:T(8,128)(2,1)}) %all-gather.5.cloned.1.call-update) | async-done | bytes 2097168 | tf_op jit(solution)/shard_map/all_gather | solution.py:86
  72.8 293.7 %while.15 = (s32[]{:T(128)}, f32[1024,1024]{1,0:T(8,128)}, f32[512,128]{1,0:T(8,128)S(1)}, f32[512,128]{1,0:T(8,128)S(1)}, s32[8]{0:T(128)S(1)}, /*index=5*/bf16...) while((s32[]{:T(128)}, f32[1024,1024]{1,0:T(8,128)}, ...), condition=%wide.region_9.10_spmd.clone, body=%wide.region_2.9_spmd.clone.sunk | while | flops 686228480 | bytes 18841836 | solution.py:74
  75.4 13.1 %pmax.9 = f32[1024]{0:T(1024)S(1)} all-reduce(f32[1024]{0:T(1024)S(1)} %get-tuple-element.203), channel_id=1, replica_groups=mesh['qrow'=8,'kcol'=4] {'qrow'}, use_global_device_ids=true, to_apply=%region_4.4 | all-reduce | flops 1024 | bytes 8192 | tf_op jit(solution)/shard_map/while/body/eval_jaxpr/pmax | solution.py:25
  91.7 12.0 %all-reduce.2 = (f32[1024]{0:T(1024)S(1)}, f32[1024]{0:T(1024)S(1)}) all-reduce(f32[1024]{0:T(1024)S(1)} %get-tuple-element.206, f32[1024]{0:T(1024)S(1)} %get-tuple-element.207), channel_id=1, replica_groups=mesh['qrow'=8,'kcol'=4] {'qrow'}, use_global_device_ids=true, to_apply=%region_8.8 | all-reduce | flops 2048 | bytes 16384 | tf_op jit(solution)/shard_map/while/body/eval_jaxpr/psum | solution.py:27
  113.4 11.8 %pmax.9 = f32[1024]{0:T(1024)S(1)} all-reduce(f32[1024]{0:T(1024)S(1)} %get-tuple-element.203), channel_id=1, replica_groups=mesh['qrow'=8,'kcol'=4] {'qrow'}, use_global_device_ids=true, to_apply=%region_4.4 | all-reduce | flops 1024 | bytes 8192 | tf_op jit(solution)/shard_map/while/body/eval_jaxpr/pmax | solution.py:25
  128.3 12.0 %all-reduce.2 = (f32[1024]{0:T(1024)S(1)}, f32[1024]{0:T(1024)S(1)}) all-reduce(f32[1024]{0:T(1024)S(1)} %get-tuple-element.206, f32[1024]{0:T(1024)S(1)} %get-tuple-element.207), channel_id=1, replica_groups=mesh['qrow'=8,'kcol'=4] {'qrow'}, use_global_device_ids=true, to_apply=%region_8.8 | all-reduce | flops 2048 | bytes 16384 | tf_op jit(solution)/shard_map/while/body/eval_jaxpr/psum | solution.py:27
  149.9 11.8 %pmax.9 = f32[1024]{0:T(1024)S(1)} all-reduce(f32[1024]{0:T(1024)S(1)} %get-tuple-element.203), channel_id=1, replica_groups=mesh['qrow'=8,'kcol'=4] {'qrow'}, use_global_device_ids=true, to_apply=%region_4.4 | all-reduce | flops 1024 | bytes 8192 | tf_op jit(solution)/shard_map/while/body/eval_jaxpr/pmax | solution.py:25
  164.8 12.0 %all-reduce.2 = (f32[1024]{0:T(1024)S(1)}, f32[1024]{0:T(1024)S(1)}) all-reduce(f32[1024]{0:T(1024)S(1)} %get-tuple-element.206, f32[1024]{0:T(1024)S(1)} %get-tuple-element.207), channel_id=1, replica_groups=mesh['qrow'=8,'kcol'=4] {'qrow'}, use_global_device_ids=true, to_apply=%region_8.8 | all-reduce | flops 2048 | bytes 16384 | tf_op jit(solution)/shard_map/while/body/eval_jaxpr/psum | solution.py:27
  186.4 11.8 %pmax.9 = f32[1024]{0:T(1024)S(1)} all-reduce(f32[1024]{0:T(1024)S(1)} %get-tuple-element.203), channel_id=1, replica_groups=mesh['qrow'=8,'kcol'=4] {'qrow'}, use_global_device_ids=true, to_apply=%region_4.4 | all-reduce | flops 1024 | bytes 8192 | tf_op jit(solution)/shard_map/while/body/eval_jaxpr/pmax | solution.py:25
  198.3 3.1 fusion.43
  201.4 12.0 %all-reduce.2 = (f32[1024]{0:T(1024)S(1)}, f32[1024]{0:T(1024)S(1)}) all-reduce(f32[1024]{0:T(1024)S(1)} %get-tuple-element.206, f32[1024]{0:T(1024)S(1)} %get-tuple-element.207), channel_id=1, replica_groups=mesh['qrow'=8,'kcol'=4] {'qrow'}, use_global_device_ids=true, to_apply=%region_8.8 | all-reduce | flops 2048 | bytes 16384 | tf_op jit(solution)/shard_map/while/body/eval_jaxpr/psum | solution.py:27
  223.0 11.8 %pmax.9 = f32[1024]{0:T(1024)S(1)} all-reduce(f32[1024]{0:T(1024)S(1)} %get-tuple-element.203), channel_id=1, replica_groups=mesh['qrow'=8,'kcol'=4] {'qrow'}, use_global_device_ids=true, to_apply=%region_4.4 | all-reduce | flops 1024 | bytes 8192 | tf_op jit(solution)/shard_map/while/body/eval_jaxpr/pmax | solution.py:25
  237.9 12.0 %all-reduce.2 = (f32[1024]{0:T(1024)S(1)}, f32[1024]{0:T(1024)S(1)}) all-reduce(f32[1024]{0:T(1024)S(1)} %get-tuple-element.206, f32[1024]{0:T(1024)S(1)} %get-tuple-element.207), channel_id=1, replica_groups=mesh['qrow'=8,'kcol'=4] {'qrow'}, use_global_device_ids=true, to_apply=%region_8.8 | all-reduce | flops 2048 | bytes 16384 | tf_op jit(solution)/shard_map/while/body/eval_jaxpr/psum | solution.py:27
  259.5 11.8 %pmax.9 = f32[1024]{0:T(1024)S(1)} all-reduce(f32[1024]{0:T(1024)S(1)} %get-tuple-element.203), channel_id=1, replica_groups=mesh['qrow'=8,'kcol'=4] {'qrow'}, use_global_device_ids=true, to_apply=%region_4.4 | all-reduce | flops 1024 | bytes 8192 | tf_op jit(solution)/shard_map/while/body/eval_jaxpr/pmax | solution.py:25
  274.4 12.0 %all-reduce.2 = (f32[1024]{0:T(1024)S(1)}, f32[1024]{0:T(1024)S(1)}) all-reduce(f32[1024]{0:T(1024)S(1)} %get-tuple-element.206, f32[1024]{0:T(1024)S(1)} %get-tuple-element.207), channel_id=1, replica_groups=mesh['qrow'=8,'kcol'=4] {'qrow'}, use_global_device_ids=true, to_apply=%region_8.8 | all-reduce | flops 2048 | bytes 16384 | tf_op jit(solution)/shard_map/while/body/eval_jaxpr/psum | solution.py:27
  296.1 11.8 %pmax.9 = f32[1024]{0:T(1024)S(1)} all-reduce(f32[1024]{0:T(1024)S(1)} %get-tuple-element.203), channel_id=1, replica_groups=mesh['qrow'=8,'kcol'=4] {'qrow'}, use_global_device_ids=true, to_apply=%region_4.4 | all-reduce | flops 1024 | bytes 8192 | tf_op jit(solution)/shard_map/while/body/eval_jaxpr/pmax | solution.py:25
  311.0 12.0 %all-reduce.2 = (f32[1024]{0:T(1024)S(1)}, f32[1024]{0:T(1024)S(1)}) all-reduce(f32[1024]{0:T(1024)S(1)} %get-tuple-element.206, f32[1024]{0:T(1024)S(1)} %get-tuple-element.207), channel_id=1, replica_groups=mesh['qrow'=8,'kcol'=4] {'qrow'}, use_global_device_ids=true, to_apply=%region_8.8 | all-reduce | flops 2048 | bytes 16384 | tf_op jit(solution)/shard_map/while/body/eval_jaxpr/psum | solution.py:27
  332.6 11.8 %pmax.9 = f32[1024]{0:T(1024)S(1)} all-reduce(f32[1024]{0:T(1024)S(1)} %get-tuple-element.203), channel_id=1, replica_groups=mesh['qrow'=8,'kcol'=4] {'qrow'}, use_global_device_ids=true, to_apply=%region_4.4 | all-reduce | flops 1024 | bytes 8192 | tf_op jit(solution)/shard_map/while/body/eval_jaxpr/pmax | solution.py:25
  347.5 12.0 %all-reduce.2 = (f32[1024]{0:T(1024)S(1)}, f32[1024]{0:T(1024)S(1)}) all-reduce(f32[1024]{0:T(1024)S(1)} %get-tuple-element.206, f32[1024]{0:T(1024)S(1)} %get-tuple-element.207), channel_id=1, replica_groups=mesh['qrow'=8,'kcol'=4] {'qrow'}, use_global_device_ids=true, to_apply=%region_8.8 | all-reduce | flops 2048 | bytes 16384 | tf_op jit(solution)/shard_map/while/body/eval_jaxpr/psum | solution.py:27
  368.4 19.4 %reduce-scatter.8.cloned.1.call-done = f32[128,128]{1,0:T(8,128)} async-done(((f32[512,128]{1,0:T(8,128)}), f32[128,128]{1,0:T(8,128)}) %reduce-scatter.8.cloned.1.call-update) | async-done | bytes 65552 | tf_op jit(solution)/shard_map/reduce_scatter | solution.py:102
  389.2 19.2 %reduce-scatter.6.cloned.1.call-done = f32[128,128]{1,0:T(8,128)} async-done(((f32[512,128]{1,0:T(8,128)}), f32[128,128]{1,0:T(8,128)}) %reduce-scatter.6.cloned.1.call-update) | async-done | bytes 65552 | tf_op jit(solution)/shard_map/reduce_scatter | solution.py:101
  409.8 51.4 %reduce-scatter.4.cloned.1.call-done = f32[128,1024]{1,0:T(8,128)} async-done(((f32[1024,1024]{1,0:T(8,128)}), f32[128,1024]{1,0:T(8,128)}) %reduce-scatter.4.cloned.1.call-update) | async-done | bytes 524304 | tf_op jit(solution)/shard_map/reduce_scatter | solution.py:99
  (93 shorter events, 106.2 us)
Async XLA Ops:
  7.2 33.4 %all-gather.3.cloned.1.call-start = ((), (), s32[]{:S(2)}) async-start(), calls=%async_computation.3 | async-start | bytes 2359296 | tf_op jit(solution)/shard_map/all_gather | solution.py:85
  7.9 62.4 %all-gather.5.cloned.1.call-start = ((), (), s32[]{:S(2)}) async-start(), calls=%async_computation.4 | async-start | bytes 2359296 | tf_op jit(solution)/shard_map/all_gather | solution.py:86
  8.6 379.1 %reduce-scatter.8.cloned.1.call-start = ((), (), s32[]{:S(2)}) async-start(), calls=%async_computation.7 | async-start | bytes 327680 | tf_op jit(solution)/shard_map/reduce_scatter | solution.py:102
  366.5 0.7 copy-start.1
  366.5 0.8 copy-start
  367.2 41.2 %reduce-scatter.6.cloned.1.call-start = ((), (), s32[]{:S(2)}) async-start(), calls=%async_computation.6 | async-start | bytes 327680 | tf_op jit(solution)/shard_map/reduce_scatter | solution.py:101
  367.8 93.5 %reduce-scatter.4.cloned.1.call-start = ((), (), s32[]{:S(2)}) async-start(), calls=%async_computation.5 | async-start | bytes 4718592 | tf_op jit(solution)/shard_map/reduce_scatter | solution.py:99
Sparse Core Ops, SparseCore 0:
  9.9 30.5 all-gather.2
  42.4 27.8 all-gather.4
  367.3 20.3 reduce-scatter.7
  390.5 17.7 reduce-scatter.5
  411.6 49.6 reduce-scatter.3
where the time goes:
time: 471 us; the launch traced here: 470 us
  blocking collectives  221 us (47%)
  waiting for transfers between devices  123 us (26%)
  matrix products  72.3 us (15%)
  other arithmetic  25.7 us (5%)
  between operations  13.8 us (3%)
  local copies, waits for them, and re-layouts  7.82 us (2%)
  loops' own time  5.62 us (1%)
    psum x8, blocking collectives, head_stats(): lax.psum((jnp.sum(raised, axis=1), jnp.sum(raised * grad_weights, axis=1)...  96.2 us
    pmax x8, blocking collectives, head_stats(): top = lax.pmax(local_top, 'qrow')  95.7 us
    reduce_scatter x1, waiting for transfers between devices, per_device(): lax.psum_scatter(query_sum, 'qrow', scatter_dimension=0, tiled=True)  51.4 us
    all_gather x1, waiting for transfers between devices, per_device(): lax.all_gather(grad_out, 'qrow', axis=0, tiled=True)  29.8 us
    dot_general x8, matrix products, per_head(): jnp.einsum('qd,kd->qk', grad_head, value_block, preferred_element_type=jn...  24.8 us
    reduce_scatter x1, waiting for transfers between devices, per_device(): lax.psum_scatter(value_sum, 'kcol', scatter_dimension=0, tiled=True)  19.4 us
    reduce_scatter x1, waiting for transfers between devices, per_device(): lax.psum_scatter(key_sum, 'kcol', scatter_dimension=0, tiled=True)  19.2 us
    convert_element_type x8, other arithmetic, per_head(): (attention * (grad_weights - delta[:, None])).astype(jnp.bfloat16)  19.1 us
  transfers between devices with their start and end apart: 5, of which 5 were waited for; matrix products, arithmetic and copies ran while one was open for 1% of the time, Pallas kernels for 0%

commit v1 on v0

v1 whole, which is shorter than its diff:
```python
import functools
import math

import jax
import jax.numpy as jnp
from jax import lax
from jax.experimental import pallas as pl
from jax.experimental.pallas import tpu as pltpu
from jax.sharding import PartitionSpec as P

HD = 128
BIG = 1e30
F32 = jnp.float32
BF16 = jnp.bfloat16
ROOT = 1.0 / math.sqrt(HD)
SCALE = ROOT / math.log(2.0)
MESH = pl.DeviceIdType.MESH


def nn(a, b):
    return lax.dot_general(a, b, (((1,), (0,)), ((), ())), preferred_element_type=F32)


def nt(a, b):
    return lax.dot_general(a, b, (((1,), (1,)), ((), ())), preferred_element_type=F32)


def tn(a, b):
    return lax.dot_general(a, b, (((0,), (0,)), ((), ())), preferred_element_type=F32)


def kernel(
    rows_count, cols_count, length, heads, tile,
    order, q_ref, k_ref, v_ref, g_ref, dq_ref, dk_ref, dv_ref,
    kv, raised, qt, gt, tops, top, total, out_t, delta, dq_t, diag,
    own_sum, chip_sum, peer_send, peer_recv, chip_recv, col_recv,
    s1, r1, s2, r2, s3, r3, s4, r4, s5, r5, s6, r6,
):
    chips = rows_count // 2
    row = lax.axis_index("qrow")
    col = lax.axis_index("kcol")
    chip = lax.div(row, 2)
    core = lax.rem(row, 2)
    peer = chip * 2 + (1 - core)
    me = row * cols_count + col
    span = cols_count * length
    subs = span // tile
    lanes = heads * length

    def other_col(k):
        return (row, lax.rem(col + k, cols_count))

    def other_chip(k):
        return (lax.rem(chip + k, chips) * 2 + core, col)

    def source_row(k, which):
        return lax.rem(chip + chips - k, chips) * 2 + which

    def target_row(k, which):
        return lax.rem(chip + k, chips) * 2 + which

    barrier = pltpu.get_barrier_semaphore()
    for k in range(1, cols_count):
        pl.semaphore_signal(barrier, inc=1, device_id=other_col(k), device_id_type=MESH)
    for k in range(1, chips):
        pl.semaphore_signal(barrier, inc=1, device_id=other_chip(k), device_id_type=MESH)
    pl.semaphore_signal(barrier, inc=1, device_id=(peer, col), device_id_type=MESH)
    own = pl.ds(pl.multiple_of(col * length, length), length)
    kv[row, own, 0:HD] = k_ref[...]
    kv[row, own, HD : 2 * HD] = v_ref[...]
    pl.semaphore_wait(barrier, cols_count + chips - 1)

    def copy_col(k):
        part = kv.at[row, own]
        return pltpu.make_async_remote_copy(
            src_ref=part, dst_ref=part, send_sem=s1.at[k], recv_sem=r1.at[k],
            device_id=other_col(k), device_id_type=MESH,
        )

    def copy_chip(k):
        return pltpu.make_async_remote_copy(
            src_ref=kv.at[row], dst_ref=kv.at[row], send_sem=s2.at[k], recv_sem=r2.at[k],
            device_id=other_chip(k), device_id_type=MESH,
        )

    def copy_core(k):
        part = kv.at[source_row(k, core)]
        return pltpu.make_async_remote_copy(
            src_ref=part, dst_ref=part, send_sem=s3.at[k], recv_sem=r3.at[k],
            device_id=(peer, col), device_id_type=MESH,
        )

    for k in range(1, cols_count):
        copy_col(k).start()

    for h in range(heads):
        cut = slice(h * HD, (h + 1) * HD)
        put = slice(h * length, (h + 1) * length)
        qt[:, put] = q_ref[:, cut].T
        gt[:, put] = g_ref[:, cut].T

    key_at = lax.broadcasted_iota(jnp.int32, (length, lanes), 0)
    row_at = lax.rem(lax.broadcasted_iota(jnp.int32, (length, lanes), 1), length)
    scores = jnp.where(key_at <= row_at, nn(k_ref[...], qt[...]), -BIG)
    first = jnp.max(scores, axis=0, keepdims=True)
    own_raised = jnp.exp2((scores - first) * SCALE)
    own_low = own_raised.astype(BF16)
    diag[...] = own_low
    top[...] = first
    tops[rows_count * subs] = first
    total[...] = jnp.sum(own_raised, axis=0, keepdims=True)
    out_t[...] = tn(v_ref[...], own_low)

    def hidden(block):
        return jnp.where(order[block] < order[me], 0.0, BIG).astype(F32)

    def forward(which):
        @pl.loop(0, subs)
        def _(sub):
            at = pl.ds(pl.multiple_of(sub * tile, tile), tile)
            scores = nn(kv[which, at, 0:HD], qt[...])
            first_block = which * cols_count + sub * (tile // length)
            old = top[...]
            new = old
            offs = []
            for b in range(tile // length):
                off = hidden(first_block + b)
                offs.append(off)
                part = scores[b * length : (b + 1) * length]
                new = jnp.maximum(new, jnp.max(part, axis=0, keepdims=True) - off)
            alpha = jnp.exp2((old - new) * SCALE)
            shift = new * SCALE
            parts = []
            add = jnp.zeros_like(old)
            for b in range(tile // length):
                part = scores[b * length : (b + 1) * length]
                up = jnp.exp2(part * SCALE - (shift + offs[b]))
                add = add + jnp.sum(up, axis=0, keepdims=True)
                parts.append(up.astype(BF16))
            low = jnp.concatenate(parts, axis=0)
            index = which * subs + sub
            raised[index] = low
            top[...] = new
            tops[index] = new
            total[...] = total[...] * alpha + add
            out_t[...] = out_t[...] * alpha + tn(kv[which, at, HD : 2 * HD], low)

    for k in range(1, cols_count):
        copy_col(k).wait_recv()
    for k in range(1, chips):
        copy_chip(k).start()

    @pl.loop(0, chips)
    def _(k):
        @pl.when(k > 0)
        def _():
            copy_chip(k).wait_recv()

        copy_core(k).start()
        forward(source_row(k, core))
        copy_core(k).wait_recv()
        forward(source_row(k, 1 - core))

    inverse = 1.0 / total[...]
    delta[...] = (
        jnp.sum(out_t[...] * gt[...].astype(F32), axis=0, keepdims=True) * inverse
    )

    def terms(values, keys, low, index):
        grad_weights = nn(values, gt[...])
        grad_low = (grad_weights - delta[...]).astype(BF16) * low
        share = jnp.exp2((tops[index] - top[...]) * SCALE) / total[...]
        scaled_q = (qt[...].astype(F32) * (share * ROOT)).astype(BF16)
        scaled_g = (gt[...].astype(F32) * share).astype(BF16)
        grad_q = tn(keys, grad_low) * (share * ROOT)
        return nt(grad_low, scaled_q), nt(low, scaled_g), grad_q

    own_dk, own_dv, own_dq = terms(v_ref[...], k_ref[...], diag[...], rows_count * subs)
    own_sum[:, 0:HD] = own_dk
    own_sum[:, HD : 2 * HD] = own_dv
    dq_t[...] = own_dq

    def backward(which, store):
        @pl.loop(0, subs)
        def _(sub):
            at = pl.ds(pl.multiple_of(sub * tile, tile), tile)
            index = which * subs + sub
            grad_k, grad_v, grad_q = terms(
                kv[which, at, HD : 2 * HD], kv[which, at, 0:HD], raised[index], index
            )
            dq_t[...] += grad_q
            store(at, grad_k, grad_v)

    def give_core(k):
        return pltpu.make_async_remote_copy(
            src_ref=peer_send.at[k], dst_ref=peer_recv.at[k],
            send_sem=s4.at[k], recv_sem=r4.at[k],
            device_id=(peer, col), device_id_type=MESH,
        )

    def give_chip(k):
        return pltpu.make_async_remote_copy(
            src_ref=peer_recv.at[k], dst_ref=chip_recv.at[k],
            send_sem=s5.at[k], recv_sem=r5.at[k],
            device_id=other_chip(k), device_id_type=MESH,
        )

    def give_col(k):
        return pltpu.make_async_remote_copy(
            src_ref=peer_recv.at[0, pl.ds(lax.rem(col + k, cols_count) * length, length)],
            dst_ref=col_recv.at[k],
            send_sem=s6.at[k], recv_sem=r6.at[k],
            device_id=other_col(k), device_id_type=MESH,
        )

    @pl.loop(0, chips)
    def _(step):
        k = lax.rem(step + 1, chips)

        def to_peer(at, grad_k, grad_v):
            peer_send[k, at, 0:HD] = grad_k.astype(BF16)
            peer_send[k, at, HD : 2 * HD] = grad_v.astype(BF16)

        backward(target_row(k, 1 - core), to_peer)
        give_core(k).start()

        def to_sum(at, grad_k, grad_v):
            chip_sum[at, 0:HD] = grad_k
            chip_sum[at, HD : 2 * HD] = grad_v

        backward(target_row(k, core), to_sum)
        give_core(k).wait_recv()
        chip_sum[...] += peer_recv[k].astype(F32)

        @pl.when(k > 0)
        def _():
            peer_recv[k] = chip_sum[...].astype(BF16)
            give_chip(k).start()

    for k in range(1, chips):
        give_chip(k).wait_recv()
        chip_sum[...] += chip_recv[k].astype(F32)
    peer_recv[0] = chip_sum[...].astype(BF16)
    for k in range(1, cols_count):
        give_col(k).start()
    for h in range(heads):
        cut = slice(h * HD, (h + 1) * HD)
        put = slice(h * length, (h + 1) * length)
        dq_ref[:, cut] = dq_t[:, put].T.astype(BF16)
    last = chip_sum[own] + own_sum[...]
    for k in range(1, cols_count):
        give_col(k).wait_recv()
        last = last + col_recv[k].astype(F32)
    dk_ref[...] = last[:, 0:HD].astype(BF16)
    dv_ref[...] = last[:, HD : 2 * HD].astype(BF16)

    for k in range(1, cols_count):
        copy_col(k).wait_send()
        give_col(k).wait_send()
    for k in range(1, chips):
        copy_chip(k).wait_send()
        give_chip(k).wait_send()
    for k in range(chips):
        copy_core(k).wait_send()
        give_core(k).wait_send()


def per_device(queries, keys, values, grad_out, block_order):
    rows_count = lax.axis_size("qrow")
    cols_count = lax.axis_size("kcol")
    length = queries.shape[0]
    heads = queries.shape[1] // HD
    chips = rows_count // 2
    span = cols_count * length
    tile = min(512, span)
    subs = span // tile
    lanes = heads * length
    vmem = pl.BlockSpec(memory_space=pltpu.VMEM)
    dma = pltpu.SemaphoreType.DMA
    return pl.pallas_call(
        functools.partial(kernel, rows_count, cols_count, length, heads, tile),
        out_shape=(
            jax.ShapeDtypeStruct(queries.shape, BF16),
            jax.ShapeDtypeStruct(keys.shape, BF16),
            jax.ShapeDtypeStruct(values.shape, BF16),
        ),
        in_specs=[pl.BlockSpec(memory_space=pltpu.SMEM)] + [vmem] * 4,
        out_specs=(vmem, vmem, vmem),
        scratch_shapes=[
            pltpu.VMEM((rows_count, span, 2 * HD), BF16),
            pltpu.VMEM((rows_count * subs, tile, lanes), BF16),
            pltpu.VMEM((HD, lanes), BF16),
            pltpu.VMEM((HD, lanes), BF16),
            pltpu.VMEM((rows_count * subs + 1, 1, lanes), F32),
            pltpu.VMEM((1, lanes), F32),
            pltpu.VMEM((1, lanes), F32),
            pltpu.VMEM((HD, lanes), F32),
            pltpu.VMEM((1, lanes), F32),
            pltpu.VMEM((HD, lanes), F32),
            pltpu.VMEM((length, lanes), BF16),
            pltpu.VMEM((length, 2 * HD), F32),
            pltpu.VMEM((span, 2 * HD), F32),
            pltpu.VMEM((chips, span, 2 * HD), BF16),
            pltpu.VMEM((chips, span, 2 * HD), BF16),
            pltpu.VMEM((chips, span, 2 * HD), BF16),
            pltpu.VMEM((cols_count, length, 2 * HD), BF16),
            dma((cols_count,)), dma((cols_count,)),
            dma((chips,)), dma((chips,)),
            dma((chips,)), dma((chips,)),
            dma((chips,)), dma((chips,)),
            dma((chips,)), dma((chips,)),
            dma((cols_count,)), dma((cols_count,)),
        ],
        compiler_params=pltpu.CompilerParams(
            collective_id=0, has_side_effects=True, vmem_limit_bytes=62 * 1024 * 1024
        ),
    )(block_order, queries, keys, values, grad_out)


def solution(mesh):
    return jax.shard_map(
        per_device,
        mesh=mesh,
        in_specs=(
            P(("qrow", "kcol"), None),
            P(("qrow", "kcol"), None),
            P(("qrow", "kcol"), None),
            P(("qrow", "kcol"), None),
            P(),
        ),
        out_specs=(P(("qrow", "kcol"), None), P(("qrow", "kcol"), None), P(("qrow", "kcol"), None)),
        check_vma=False,
    )
```

time: 471 us -> 58.4 us (0.12)
  blocking collectives: 221 us -> 0 us
  waiting for transfers between devices: 123 us -> 0 us
  matrix products: 72.3 us -> 0 us
  Pallas kernels: 0 us -> 54.1 us
  other arithmetic: 25.7 us -> 0 us
  between operations: 13.8 us -> 0.65 us
  loops' own time: 5.62 us -> 0 us
  local copies, waits for them, and re-layouts: 7.82 us -> 3.06 us
    psum x8 -> x0, blocking collectives: 96.2 us -> none  [head_stats(): lax.psum((jnp.sum(raised, axis=1), jnp.sum(raised * grad_weights, axis=1)...]
    pmax x8 -> x0, blocking collectives: 95.7 us -> none  [head_stats(): top = lax.pmax(local_top, 'qrow')]
    reduce_scatter x3 -> x0, waiting for transfers between devices: 90 us -> none  [the longest x1 51.4 us: per_device(): lax.psum_scatter(query_sum, 'qrow', scatter_dimension=0, tiled=True)]
    dot_general x40 -> x0, matrix products: 72.3 us -> none  [the longest x8 24.8 us: per_head(): jnp.einsum('qd,kd->qk', grad_head, value_block, preferred_element_type=jn...]
    pallas_call x0 -> x1, Pallas kernels: none -> 54.1 us  [per_device(): pl.pallas_call(functools.partial(kernel, rows_count, cols_count, length,...]
    all_gather x2 -> x0, waiting for transfers between devices: 30.6 us -> none  [the longest x1 29.8 us: per_device(): lax.all_gather(grad_out, 'qrow', axis=0, tiled=True)]
    all_gather x2 -> x0, blocking collectives: 29.1 us -> none  [the longest x1 15.3 us: per_device(): lax.all_gather(keys, 'kcol', axis=0, tiled=True)]
    convert_element_type x11 -> x0, other arithmetic: 23.8 us -> none  [the longest x8 19.1 us: per_head(): (attention * (grad_weights - delta[:, None])).astype(jnp.bfloat16)]
  transfers between devices with their start and end apart: 5 -> 0, of which waited for: 5 -> 0; matrix products, arithmetic and copies ran while one was open for 1% -> 0% of each run, Pallas kernels for 0% -> 0%
where the time goes in v1:
time: 58.4 us; the launch traced here: 57.8 us
  Pallas kernels  54.1 us (93%)
  local copies, waits for them, and re-layouts  3.06 us (5%)
  between operations  0.65 us (1%)
    pallas_call x1, Pallas kernels, per_device(): pl.pallas_call(functools.partial(kernel, rows_count, cols_count, length,...  54.1 us
    unnamed x7, local copies, waits for them, and re-layouts  3.06 us

profile of v1, /device:TPU:0, one launch (start us, length us, event | category | flops | bytes accessed | tf_op | source)
XLA Modules:
  0.0 57.8 jit_solution(6053804797116197238)
XLA Ops:
  0.6 54.1 %shard_map.76 = (bf16[128,1024]{1,0:T(8,128)(2,1)}, bf16[128,128]{1,0:T(8,128)(2,1)}, bf16[128,128]{1,0:T(8,128)(2,1)}) custom-call(s32[32]{0:T(128)} %order.1, bf16[128,1024]{1,0:T(8,128)(2,1)} %q_ref.1, bf16[128,128]{1,0:T(8,128)(2,1)} %k_ref.1, bf16[128,128]{1,0:T(8,128)(2,1)} %v_ref.1, bf16[128,1024]{1,0:T(8,128)(2,1)} %g_ref.1), custom_call_target="tpu_custom_call" | custom-call | tf_op jit(solution)/shard_map/pallas_call | solution.py:280
  54.7 0.0 copy-start.1
  54.8 1.7 %copy.11 = bf16[128,1024]{1,0:T(8,128)(2,1)} copy(bf16[128,1024]{1,0:T(8,128)(2,1)} %get-tuple-element.6) | data formatting | bytes 524288
  56.4 0.0 copy-done.1
  56.4 0.0 copy-start
  56.4 0.6 %copy.12 = bf16[128,128]{1,0:T(8,128)(2,1)} copy(bf16[128,128]{1,0:T(8,128)(2,1)S(1)} %copy-done.1) | data formatting | bytes 65536
  57.1 0.2 copy-done
  57.2 0.6 %copy.13 = bf16[128,128]{1,0:T(8,128)(2,1)} copy(bf16[128,128]{1,0:T(8,128)(2,1)S(1)} %copy-done) | data formatting | bytes 65536
Async XLA Ops:
  54.7 1.7 %copy-start.1 = (bf16[128,128]{1,0:T(8,128)(2,1)S(1)}, bf16[128,128]{1,0:T(8,128)(2,1)}, u32[]{:S(2)}) copy-start(bf16[128,128]{1,0:T(8,128)(2,1)} %get-tuple-element.7) | copy-start | bytes 98308
  56.4 0.8 %copy-start = (bf16[128,128]{1,0:T(8,128)(2,1)S(1)}, bf16[128,128]{1,0:T(8,128)(2,1)}, u32[]{:S(2)}) copy-start(bf16[128,128]{1,0:T(8,128)(2,1)} %get-tuple-element.8) | copy-start | bytes 98308

commit v2 on v1

v2 whole, which is shorter than its diff:
```python
import functools
import math

import jax
import jax.numpy as jnp
from jax import lax
from jax.experimental import pallas as pl
from jax.experimental.pallas import tpu as pltpu
from jax.sharding import PartitionSpec as P

HD = 128
BIG = 1e30
F32 = jnp.float32
BF16 = jnp.bfloat16
ROOT = 1.0 / math.sqrt(HD)
SCALE = ROOT / math.log(2.0)
MESH = pl.DeviceIdType.MESH


def nn(a, b):
    return lax.dot_general(a, b, (((1,), (0,)), ((), ())), preferred_element_type=F32)


def nt(a, b):
    return lax.dot_general(a, b, (((1,), (1,)), ((), ())), preferred_element_type=F32)


def tn(a, b):
    return lax.dot_general(a, b, (((0,), (0,)), ((), ())), preferred_element_type=F32)


def kernel(
    rows_count, cols_count, length, heads, tile,
    order, q_ref, k_ref, v_ref, g_ref, dq_ref, dk_ref, dv_ref,
    kv, raised, qt, gt, tops, top, total, out_t, delta, dq_t, diag,
    own_sum, chip_sum, keep, peer_send, peer_recv, chip_recv, col_send, col_recv,
    s1, r1, s2, r2, s3, r3, s4, r4, s5, r5, s6, r6,
):
    chips = rows_count // 2
    row = lax.axis_index("qrow")
    col = lax.axis_index("kcol")
    chip = lax.div(row, 2)
    core = lax.rem(row, 2)
    far = 1 - core
    peer = chip * 2 + far
    me = row * cols_count + col
    span = chips * length
    subs = span // tile
    lanes = heads * length

    def later_col(k):
        return lax.rem(col + k, cols_count)

    def earlier_col(k):
        return lax.rem(col + cols_count - k, cols_count)

    def later_chip(c):
        return lax.rem(chip + c, chips)

    def earlier_chip(c):
        return lax.rem(chip + chips - c, chips)

    def piece(c):
        return pl.ds(pl.multiple_of(c * length, length), length)

    barrier = pltpu.get_barrier_semaphore()
    partners = [(row, later_col(k)) for k in range(1, cols_count)]
    partners += [(later_chip(c) * 2 + core, col) for c in range(1, chips)]
    partners += [(peer, col)]
    for partner in partners:
        pl.semaphore_signal(barrier, inc=1, device_id=partner, device_id_type=MESH)
    own = piece(chip)
    kv[col, core, own, 0:HD] = k_ref[...]
    kv[col, core, own, HD : 2 * HD] = v_ref[...]

    for h in range(heads):
        cut = slice(h * HD, (h + 1) * HD)
        put = slice(h * length, (h + 1) * length)
        qt[:, put] = q_ref[:, cut].T
        gt[:, put] = g_ref[:, cut].T

    pl.semaphore_wait(barrier, len(partners))

    def copy_col(k):
        part = kv.at[col, core, own]
        return pltpu.make_async_remote_copy(
            src_ref=part, dst_ref=part, send_sem=s1.at[k], recv_sem=r1.at[k],
            device_id=(row, later_col(k)), device_id_type=MESH,
        )

    def copy_chip(k, c):
        part = kv.at[earlier_col(k), core, own]
        return pltpu.make_async_remote_copy(
            src_ref=part, dst_ref=part, send_sem=s2.at[k, c], recv_sem=r2.at[k, c],
            device_id=(later_chip(c) * 2 + core, col), device_id_type=MESH,
        )

    def copy_core(k, c):
        part = kv.at[earlier_col(k), core, piece(earlier_chip(c))]
        return pltpu.make_async_remote_copy(
            src_ref=part, dst_ref=part, send_sem=s3.at[k, c], recv_sem=r3.at[k, c],
            device_id=(peer, col), device_id_type=MESH,
        )

    def spread(k):
        for c in range(1, chips):
            copy_chip(k, c).start()
        copy_core(k, 0).start()

    for k in range(1, cols_count):
        copy_col(k).start()
    spread(0)

    key_at = lax.broadcasted_iota(jnp.int32, (length, lanes), 0)
    row_at = lax.rem(lax.broadcasted_iota(jnp.int32, (length, lanes), 1), length)
    scores = jnp.where(key_at <= row_at, nn(k_ref[...], qt[...]), -BIG)
    first = jnp.max(scores, axis=0, keepdims=True)
    own_raised = jnp.exp2((scores - first) * SCALE)
    own_low = own_raised.astype(BF16)
    diag[...] = own_low
    top[...] = first
    tops[2 * cols_count * subs] = first
    total[...] = jnp.sum(own_raised, axis=0, keepdims=True)
    out_t[...] = tn(v_ref[...], own_low)

    def forward(key_col, which):
        @pl.loop(0, subs)
        def _(sub):
            at = pl.ds(pl.multiple_of(sub * tile, tile), tile)
            scores = nn(kv[key_col, which, at, 0:HD], qt[...])
            old = top[...]
            new = old
            offs = []
            for b in range(tile // length):
                block = ((sub * (tile // length) + b) * 2 + which) * cols_count + key_col
                off = jnp.where(order[block] < order[me], 0.0, BIG).astype(F32)
                offs.append(off)
                part = scores[b * length : (b + 1) * length]
                new = jnp.maximum(new, jnp.max(part, axis=0, keepdims=True) - off)
            alpha = jnp.exp2((old - new) * SCALE)
            shift = new * SCALE
            parts = []
            add = jnp.zeros_like(old)
            for b in range(tile // length):
                part = scores[b * length : (b + 1) * length]
                up = jnp.exp2(part * SCALE - (shift + offs[b]))
                add = add + jnp.sum(up, axis=0, keepdims=True)
                parts.append(up.astype(BF16))
            low = jnp.concatenate(parts, axis=0)
            index = (key_col * 2 + which) * subs + sub
            raised[index] = low
            top[...] = new
            tops[index] = new
            total[...] = total[...] * alpha + add
            out_t[...] = out_t[...] * alpha + tn(kv[key_col, which, at, HD : 2 * HD], low)

    @pl.loop(0, cols_count)
    def _(k):
        @pl.when(k < cols_count - 1)
        def _():
            copy_col(k + 1).wait_recv()
            spread(k + 1)

        for c in range(1, chips):
            copy_chip(k, c).wait_recv()
            copy_core(k, c).start()
        forward(earlier_col(k), core)
        for c in range(chips):
            copy_core(k, c).wait_recv()
        forward(earlier_col(k), far)

    inverse = 1.0 / total[...]
    delta[...] = (
        jnp.sum(out_t[...] * gt[...].astype(F32), axis=0, keepdims=True) * inverse
    )

    def terms(values, keys, low, index):
        grad_weights = nn(values, gt[...])
        grad_low = (grad_weights - delta[...]).astype(BF16) * low
        share = jnp.exp2((tops[index] - top[...]) * SCALE) / total[...]
        scaled_q = (qt[...].astype(F32) * (share * ROOT)).astype(BF16)
        scaled_g = (gt[...].astype(F32) * share).astype(BF16)
        grad_q = tn(keys, grad_low) * (share * ROOT)
        return nt(grad_low, scaled_q), nt(low, scaled_g), grad_q

    dq_t[...] = jnp.zeros_like(dq_t)

    def backward(key_col, which, store):
        @pl.loop(0, subs)
        def _(sub):
            at = pl.ds(pl.multiple_of(sub * tile, tile), tile)
            index = (key_col * 2 + which) * subs + sub
            grad_k, grad_v, grad_q = terms(
                kv[key_col, which, at, HD : 2 * HD],
                kv[key_col, which, at, 0:HD],
                raised[index],
                index,
            )
            dq_t[...] += grad_q
            store(at, grad_k, grad_v)

    def give_core(k):
        return pltpu.make_async_remote_copy(
            src_ref=peer_send.at[k], dst_ref=peer_recv.at[k],
            send_sem=s4.at[k], recv_sem=r4.at[k],
            device_id=(peer, col), device_id_type=MESH,
        )

    def give_chip(k, c):
        return pltpu.make_async_remote_copy(
            src_ref=peer_recv.at[k, piece(later_chip(c))], dst_ref=chip_recv.at[k, c],
            send_sem=s5.at[k, c], recv_sem=r5.at[k, c],
            device_id=(later_chip(c) * 2 + core, col), device_id_type=MESH,
        )

    def give_col(k):
        return pltpu.make_async_remote_copy(
            src_ref=col_send.at[k], dst_ref=col_recv.at[k],
            send_sem=s6.at[k], recv_sem=r6.at[k],
            device_id=(row, later_col(k)), device_id_type=MESH,
        )

    def column_sum(k):
        result = keep[k]
        for c in range(1, chips):
            give_chip(k, c).wait_recv()
            result = result + chip_recv[k, c].astype(F32)
        return result

    def pass_on(k):
        col_send[k] = column_sum(k).astype(BF16)
        give_col(k).start()

    @pl.loop(0, cols_count)
    def _(step):
        k = lax.rem(step + 1, cols_count)

        def to_peer(at, grad_k, grad_v):
            peer_send[k, at, 0:HD] = grad_k.astype(BF16)
            peer_send[k, at, HD : 2 * HD] = grad_v.astype(BF16)

        backward(later_col(k), far, to_peer)
        give_core(k).start()

        def to_sum(at, grad_k, grad_v):
            chip_sum[at, 0:HD] = grad_k
            chip_sum[at, HD : 2 * HD] = grad_v

        backward(later_col(k), core, to_sum)
        give_core(k).wait_recv()
        keep[k] = chip_sum[own] + peer_recv[k, own].astype(F32)
        peer_recv[k] = (chip_sum[...] + peer_recv[k].astype(F32)).astype(BF16)
        for c in range(1, chips):
            give_chip(k, c).start()

        @pl.when(step > 1)
        def _():
            pass_on(step - 1)

    own_dk, own_dv, own_dq = terms(
        v_ref[...], k_ref[...], diag[...], 2 * cols_count * subs
    )
    own_sum[:, 0:HD] = own_dk
    own_sum[:, HD : 2 * HD] = own_dv
    dq_t[...] += own_dq
    for k in range(max(1, cols_count - 1), cols_count):
        pass_on(k)
    for h in range(heads):
        cut = slice(h * HD, (h + 1) * HD)
        put = slice(h * length, (h + 1) * length)
        dq_ref[:, cut] = dq_t[:, put].T.astype(BF16)
    last = own_sum[...] + column_sum(0)
    for k in range(1, cols_count):
        give_col(k).wait_recv()
        last = last + col_recv[k].astype(F32)
    dk_ref[...] = last[:, 0:HD].astype(BF16)
    dv_ref[...] = last[:, HD : 2 * HD].astype(BF16)

    for k in range(1, cols_count):
        copy_col(k).wait_send()
        give_col(k).wait_send()
    for k in range(cols_count):
        give_core(k).wait_send()
        copy_core(k, 0).wait_send()
        for c in range(1, chips):
            copy_chip(k, c).wait_send()
            copy_core(k, c).wait_send()
            give_chip(k, c).wait_send()


def per_device(queries, keys, values, grad_out, block_order):
    rows_count = lax.axis_size("qrow")
    cols_count = lax.axis_size("kcol")
    length = queries.shape[0]
    heads = queries.shape[1] // HD
    chips = rows_count // 2
    span = chips * length
    tile = min(512, span)
    subs = span // tile
    lanes = heads * length
    vmem = pl.BlockSpec(memory_space=pltpu.VMEM)
    dma = pltpu.SemaphoreType.DMA
    return pl.pallas_call(
        functools.partial(kernel, rows_count, cols_count, length, heads, tile),
        out_shape=(
            jax.ShapeDtypeStruct(queries.shape, BF16),
            jax.ShapeDtypeStruct(keys.shape, BF16),
            jax.ShapeDtypeStruct(values.shape, BF16),
        ),
        in_specs=[pl.BlockSpec(memory_space=pltpu.SMEM)] + [vmem] * 4,
        out_specs=(vmem, vmem, vmem),
        scratch_shapes=[
            pltpu.VMEM((cols_count, 2, span, 2 * HD), BF16),
            pltpu.VMEM((2 * cols_count * subs, tile, lanes), BF16),
            pltpu.VMEM((HD, lanes), BF16),
            pltpu.VMEM((HD, lanes), BF16),
            pltpu.VMEM((2 * cols_count * subs + 1, 1, lanes), F32),
            pltpu.VMEM((1, lanes), F32),
            pltpu.VMEM((1, lanes), F32),
            pltpu.VMEM((HD, lanes), F32),
            pltpu.VMEM((1, lanes), F32),
            pltpu.VMEM((HD, lanes), F32),
            pltpu.VMEM((length, lanes), BF16),
            pltpu.VMEM((length, 2 * HD), F32),
            pltpu.VMEM((span, 2 * HD), F32),
            pltpu.VMEM((cols_count, length, 2 * HD), F32),
            pltpu.VMEM((cols_count, span, 2 * HD), BF16),
            pltpu.VMEM((cols_count, span, 2 * HD), BF16),
            pltpu.VMEM((cols_count, chips, length, 2 * HD), BF16),
            pltpu.VMEM((cols_count, length, 2 * HD), BF16),
            pltpu.VMEM((cols_count, length, 2 * HD), BF16),
            dma((cols_count,)), dma((cols_count,)),
            dma((cols_count, chips)), dma((cols_count, chips)),
            dma((cols_count, chips)), dma((cols_count, chips)),
            dma((cols_count,)), dma((cols_count,)),
            dma((cols_count, chips)), dma((cols_count, chips)),
            dma((cols_count,)), dma((cols_count,)),
        ],
        compiler_params=pltpu.CompilerParams(
            collective_id=0, has_side_effects=True, vmem_limit_bytes=62 * 1024 * 1024
        ),
    )(block_order, queries, keys, values, grad_out)


def solution(mesh):
    return jax.shard_map(
        per_device,
        mesh=mesh,
        in_specs=(
            P(("qrow", "kcol"), None),
            P(("qrow", "kcol"), None),
            P(("qrow", "kcol"), None),
            P(("qrow", "kcol"), None),
            P(),
        ),
        out_specs=(P(("qrow", "kcol"), None), P(("qrow", "kcol"), None), P(("qrow", "kcol"), None)),
        check_vma=False,
    )
```

time: 58.4 us -> 47.8 us (0.82)
  Pallas kernels: 54.1 us -> 43.8 us
    pallas_call x1, Pallas kernels: 54.1 us -> 43.8 us  [per_device(): pl.pallas_call(functools.partial(kernel, rows_count, cols_count, length,...]
where the time goes in v2:
time: 47.8 us; the launch traced here: 47.5 us
  Pallas kernels  43.8 us (92%)
  local copies, waits for them, and re-layouts  3.06 us (6%)
  between operations  0.65 us (1%)
    pallas_call x1, Pallas kernels, per_device(): pl.pallas_call(functools.partial(kernel, rows_count, cols_count, length,...  43.8 us
    unnamed x7, local copies, waits for them, and re-layouts  3.06 us

profile of v2, /device:TPU:0, one launch (start us, length us, event | category | flops | bytes accessed | tf_op | source)
XLA Modules:
  0.0 47.5 jit_solution(11235776765990815784)
XLA Ops:
  0.6 43.8 %shard_map.76 = (bf16[128,1024]{1,0:T(8,128)(2,1)}, bf16[128,128]{1,0:T(8,128)(2,1)}, bf16[128,128]{1,0:T(8,128)(2,1)}) custom-call(s32[32]{0:T(128)} %order.1, bf16[128,1024]{1,0:T(8,128)(2,1)} %q_ref.1, bf16[128,128]{1,0:T(8,128)(2,1)} %k_ref.1, bf16[128,128]{1,0:T(8,128)(2,1)} %v_ref.1, bf16[128,1024]{1,0:T(8,128)(2,1)} %g_ref.1), custom_call_target="tpu_custom_call" | custom-call | tf_op jit(solution)/shard_map/pallas_call | solution.py:303
  44.5 0.0 copy-start.1
  44.5 1.7 %copy.11 = bf16[128,1024]{1,0:T(8,128)(2,1)} copy(bf16[128,1024]{1,0:T(8,128)(2,1)} %get-tuple-element.6) | data formatting | bytes 524288
  46.2 0.0 copy-done.1
  46.2 0.0 copy-start
  46.2 0.6 %copy.12 = bf16[128,128]{1,0:T(8,128)(2,1)} copy(bf16[128,128]{1,0:T(8,128)(2,1)S(1)} %copy-done.1) | data formatting | bytes 65536
  46.8 0.2 copy-done
  46.9 0.6 %copy.13 = bf16[128,128]{1,0:T(8,128)(2,1)} copy(bf16[128,128]{1,0:T(8,128)(2,1)S(1)} %copy-done) | data formatting | bytes 65536
Async XLA Ops:
  44.5 1.7 %copy-start.1 = (bf16[128,128]{1,0:T(8,128)(2,1)S(1)}, bf16[128,128]{1,0:T(8,128)(2,1)}, u32[]{:S(2)}) copy-start(bf16[128,128]{1,0:T(8,128)(2,1)} %get-tuple-element.7) | copy-start | bytes 98308
  46.2 0.8 %copy-start = (bf16[128,128]{1,0:T(8,128)(2,1)S(1)}, bf16[128,128]{1,0:T(8,128)(2,1)}, u32[]{:S(2)}) copy-start(bf16[128,128]{1,0:T(8,128)(2,1)} %get-tuple-element.8) | copy-start | bytes 98308

commit v3 on v2

--- a/solution.py
+++ b/solution.py
@@ -54,10 +54,18 @@
     def earlier_col(k):
         return lax.rem(col + cols_count - k, cols_count)
 
+    square = chips == 4
+    far_x = chip + 1 - 2 * lax.rem(chip, 2)
+    far_y = chip + 2 - 4 * lax.div(chip, 2)
+
     def later_chip(c):
+        if square:
+            return (chip, far_x, far_y, 3 - chip)[c]
         return lax.rem(chip + c, chips)
 
     def earlier_chip(c):
+        if square:
+            return (chip, far_x, far_y, 3 - chip)[c]
         return lax.rem(chip + chips - c, chips)
 
     def piece(c):
@@ -102,8 +110,21 @@
             device_id=(peer, col), device_id_type=MESH,
         )
 
+    def copy_corner(k):
+        turn = lax.rem(k, 2)
+        source = (1 - turn) * far_x + turn * far_y
+        target = (1 - turn) * far_y + turn * far_x
+        part = kv.at[earlier_col(k), core, piece(source)]
+        return pltpu.make_async_remote_copy(
+            src_ref=part, dst_ref=part, send_sem=s2.at[k, 3], recv_sem=r2.at[k, 3],
+            device_id=(target * 2 + core, col), device_id_type=MESH,
+        )
+
+    def send_chip(k, c):
+        return copy_corner(k) if square and c == 3 else copy_chip(k, c)
+
     def spread(k):
-        for c in range(1, chips):
+        for c in range(1, 3 if square else chips):
             copy_chip(k, c).start()
         copy_core(k, 0).start()
 
@@ -161,9 +182,18 @@
             copy_col(k + 1).wait_recv()
             spread(k + 1)
 
-        for c in range(1, chips):
-            copy_chip(k, c).wait_recv()
-            copy_core(k, c).start()
+        if square:
+            copy_chip(k, 1).wait_recv()
+            copy_chip(k, 2).wait_recv()
+            copy_corner(k).start()
+            copy_core(k, 1).start()
+            copy_core(k, 2).start()
+            copy_corner(k).wait_recv()
+            copy_core(k, 3).start()
+        else:
+            for c in range(1, chips):
+                copy_chip(k, c).wait_recv()
+                copy_core(k, c).start()
         forward(earlier_col(k), core)
         for c in range(chips):
             copy_core(k, c).wait_recv()
@@ -283,7 +313,7 @@
         give_core(k).wait_send()
         copy_core(k, 0).wait_send()
         for c in range(1, chips):
-            copy_chip(k, c).wait_send()
+            send_chip(k, c).wait_send()
             copy_core(k, c).wait_send()
             give_chip(k, c).wait_send()
 

time: 47.8 us -> 59.8 us (1.25)
  Pallas kernels: 43.8 us -> 55.9 us
    pallas_call x1, Pallas kernels: 43.8 us -> 55.9 us  [per_device(): pl.pallas_call(functools.partial(kernel, rows_count, cols_count, length,...]
where the time goes in v3:
time: 59.8 us; the launch traced here: 59.6 us
  Pallas kernels  55.9 us (93%)
  local copies, waits for them, and re-layouts  3.06 us (5%)
  between operations  0.65 us (1%)
    pallas_call x1, Pallas kernels, per_device(): pl.pallas_call(functools.partial(kernel, rows_count, cols_count, length,...  55.9 us
    unnamed x7, local copies, waits for them, and re-layouts  3.06 us

profile of v3, /device:TPU:0, one launch (start us, length us, event | category | flops | bytes accessed | tf_op | source)
XLA Modules:
  0.0 59.6 jit_solution(10484734776469554179)
XLA Ops:
  0.6 55.9 %shard_map.76 = (bf16[128,1024]{1,0:T(8,128)(2,1)}, bf16[128,128]{1,0:T(8,128)(2,1)}, bf16[128,128]{1,0:T(8,128)(2,1)}) custom-call(s32[32]{0:T(128)} %order.1, bf16[128,1024]{1,0:T(8,128)(2,1)} %q_ref.1, bf16[128,128]{1,0:T(8,128)(2,1)} %k_ref.1, bf16[128,128]{1,0:T(8,128)(2,1)} %v_ref.1, bf16[128,1024]{1,0:T(8,128)(2,1)} %g_ref.1), custom_call_target="tpu_custom_call" | custom-call | tf_op jit(solution)/shard_map/pallas_call | solution.py:333
  56.5 0.0 copy-start.1
  56.5 1.7 %copy.11 = bf16[128,1024]{1,0:T(8,128)(2,1)} copy(bf16[128,1024]{1,0:T(8,128)(2,1)} %get-tuple-element.6) | data formatting | bytes 524288
  58.2 0.0 copy-done.1
  58.2 0.0 copy-start
  58.2 0.6 %copy.12 = bf16[128,128]{1,0:T(8,128)(2,1)} copy(bf16[128,128]{1,0:T(8,128)(2,1)S(1)} %copy-done.1) | data formatting | bytes 65536
  58.8 0.2 copy-done
  59.0 0.6 %copy.13 = bf16[128,128]{1,0:T(8,128)(2,1)} copy(bf16[128,128]{1,0:T(8,128)(2,1)S(1)} %copy-done) | data formatting | bytes 65536
Async XLA Ops:
  56.5 1.7 %copy-start.1 = (bf16[128,128]{1,0:T(8,128)(2,1)S(1)}, bf16[128,128]{1,0:T(8,128)(2,1)}, u32[]{:S(2)}) copy-start(bf16[128,128]{1,0:T(8,128)(2,1)} %get-tuple-element.7) | copy-start | bytes 98308
  58.2 0.8 %copy-start = (bf16[128,128]{1,0:T(8,128)(2,1)S(1)}, bf16[128,128]{1,0:T(8,128)(2,1)}, u32[]{:S(2)}) copy-start(bf16[128,128]{1,0:T(8,128)(2,1)} %get-tuple-element.8) | copy-start | bytes 98308

commit v4 on v2

--- a/solution.py
+++ b/solution.py
@@ -154,13 +154,13 @@
             total[...] = total[...] * alpha + add
             out_t[...] = out_t[...] * alpha + tn(kv[key_col, which, at, HD : 2 * HD], low)
 
+    @pl.loop(1, cols_count)
+    def _(k):
+        copy_col(k).wait_recv()
+        spread(k)
+
     @pl.loop(0, cols_count)
     def _(k):
-        @pl.when(k < cols_count - 1)
-        def _():
-            copy_col(k + 1).wait_recv()
-            spread(k + 1)
-
         for c in range(1, chips):
             copy_chip(k, c).wait_recv()
             copy_core(k, c).start()

time: 47.8 us -> 46.5 us (0.973)
  Pallas kernels: 43.8 us -> 42.5 us
    pallas_call x1, Pallas kernels: 43.8 us -> 42.5 us  [per_device(): pl.pallas_call(functools.partial(kernel, rows_count, cols_count, length,...]
where the time goes in v4:
time: 46.5 us; the launch traced here: 46.2 us
  Pallas kernels  42.5 us (91%)
  local copies, waits for them, and re-layouts  3.06 us (7%)
  between operations  0.65 us (1%)
    pallas_call x1, Pallas kernels, per_device(): pl.pallas_call(functools.partial(kernel, rows_count, cols_count, length,...  42.5 us
    unnamed x7, local copies, waits for them, and re-layouts  3.06 us

profile of v4, /device:TPU:0, one launch (start us, length us, event | category | flops | bytes accessed | tf_op | source)
XLA Modules:
  0.0 46.2 jit_solution(4132925395844513572)
XLA Ops:
  0.6 42.5 %shard_map.76 = (bf16[128,1024]{1,0:T(8,128)(2,1)}, bf16[128,128]{1,0:T(8,128)(2,1)}, bf16[128,128]{1,0:T(8,128)(2,1)}) custom-call(s32[32]{0:T(128)} %order.1, bf16[128,1024]{1,0:T(8,128)(2,1)} %q_ref.1, bf16[128,128]{1,0:T(8,128)(2,1)} %k_ref.1, bf16[128,128]{1,0:T(8,128)(2,1)} %v_ref.1, bf16[128,1024]{1,0:T(8,128)(2,1)} %g_ref.1), custom_call_target="tpu_custom_call" | custom-call | tf_op jit(solution)/shard_map/pallas_call | solution.py:303
  43.2 0.0 copy-start.1
  43.2 1.7 %copy.11 = bf16[128,1024]{1,0:T(8,128)(2,1)} copy(bf16[128,1024]{1,0:T(8,128)(2,1)} %get-tuple-element.6) | data formatting | bytes 524288
  44.8 0.0 copy-done.1
  44.9 0.0 copy-start
  44.9 0.6 %copy.12 = bf16[128,128]{1,0:T(8,128)(2,1)} copy(bf16[128,128]{1,0:T(8,128)(2,1)S(1)} %copy-done.1) | data formatting | bytes 65536
  45.5 0.2 copy-done
  45.6 0.6 %copy.13 = bf16[128,128]{1,0:T(8,128)(2,1)} copy(bf16[128,128]{1,0:T(8,128)(2,1)S(1)} %copy-done) | data formatting | bytes 65536
Async XLA Ops:
  43.2 1.7 %copy-start.1 = (bf16[128,128]{1,0:T(8,128)(2,1)S(1)}, bf16[128,128]{1,0:T(8,128)(2,1)}, u32[]{:S(2)}) copy-start(bf16[128,128]{1,0:T(8,128)(2,1)} %get-tuple-element.7) | copy-start | bytes 98308
  44.9 0.8 %copy-start = (bf16[128,128]{1,0:T(8,128)(2,1)S(1)}, bf16[128,128]{1,0:T(8,128)(2,1)}, u32[]{:S(2)}) copy-start(bf16[128,128]{1,0:T(8,128)(2,1)} %get-tuple-element.8) | copy-start | bytes 98308
